TPU v7x, 256 devices: a whole 4x4x8 slice. The times are simulated.
256 devices in a mesh: region: 128 (over x, z, y), batch: 2 (over core).
Axes of the slice: x: 4, y: 4, z: 8, core: 2. Of those that a mesh axis runs over, the one named last changes fastest.
Arguments:
- child_pixels: int32 [256, 1024], P('region', 'batch'), may hold values from 0 to 255
- parent_pixels: int32 [128, 1024], P('region', 'batch'), may hold values from 0 to 255
- child_leaf: bfloat16 [256, 1024, 256], P('region'), may hold values from -9 to 310
- parent_leaf: bfloat16 [128, 1024, 256], P('region'), may hold values from -9 to 9
- edge_weights: bfloat16 [256, 1024, 1024], P('region'), may hold values from 1.3671875e-08 to 0.12890625
- parent_of: int32 [256], replicated, may hold values from 0 to 127, as said below
- parent_flows: bfloat16 [128, 1024, 1024], P('region', 'batch'), may hold values from 0.049804688 to 1
Outputs:
- parent_ll: float32 [128, 1024, 1024], P('region', 'batch')
- child_flows: bfloat16 [256, 1024, 1024], P('region', 'batch')
- new_weights: bfloat16 [256, 1024, 1024], P('region', 'batch')
Inputs may be any that keep to these rules, and one draw needn't show every extreme that they name: `parent_of`: child c's parent is c // 2 - 1, c // 2 or c // 2 + 1.
All inputs are finite; a program needn't handle non-finite values.
Results may differ from a plain program's by a relative error of at most 0.012.
Values may be sent and summed in bfloat16 or wider, within the bound.
No kernel may reach another device: no remote copies, remote signals or barrier semaphores. Data moves between devices by JAX's collectives and lax.ppermute only.
A program may use at most 128 MiB of HBM per device.

v0:
```python
import functools

import jax
import jax.numpy as jnp
from jax import lax
from jax.experimental import pallas as pl
from jax.experimental.pallas import tpu as pltpu
from jax.sharding import PartitionSpec as P

PRIOR = 0.05
STRIP = 128
F32, BF16 = jnp.float32, jnp.bfloat16
MIB = 2**20


def log_softmax_by_value(leaf):
    logits = jnp.transpose(leaf.astype(F32))
    top = jnp.max(logits, axis=0, keepdims=True)
    logits = logits - top
    return logits - jnp.log(jnp.sum(jnp.exp(logits), axis=0, keepdims=True))


def one_hot_rows(pixels, values):
    rows = lax.broadcasted_iota(jnp.int32, (values, pixels.shape[1]), 0)
    return jnp.where(rows == pixels, 1.0, 0.0).astype(F32)


def one_hot(pixels, values):
    count = pixels.shape[1]
    column = jnp.transpose(jnp.broadcast_to(pixels.astype(F32), (8, count)))[:, :1]
    columns = lax.broadcasted_iota(jnp.int32, (count, values), 1).astype(F32)
    return jnp.where(columns == column, 1.0, 0.0).astype(BF16)


def dot(a, b):
    return jnp.dot(a, b, preferred_element_type=F32)


def dot_t(a, b):
    return lax.dot_general(a, b, (((1,), (1,)), ((), ())), preferred_element_type=F32)


def call(kernel, name, grid, in_specs, out_specs, out_shape, args, flops, scalars=1, vmem=26, **more):
    return pl.pallas_call(
        kernel,
        grid_spec=pltpu.PrefetchScalarGridSpec(
            num_scalar_prefetch=scalars,
            grid=grid,
            in_specs=in_specs,
            out_specs=out_specs,
            scratch_shapes=more.pop("scratch", ()),
        ),
        out_shape=out_shape,
        compiler_params=pltpu.CompilerParams(vmem_limit_bytes=vmem * MIB),
        cost_estimate=pl.CostEstimate(flops=flops // 10**6, bytes_accessed=8, transcendentals=0),
        name=name,
        **more,
    )(*args)


def shape(*dims, dtype=BF16):
    return jax.ShapeDtypeStruct(dims, dtype)


TOKEN = shape(8, 128, dtype=F32)


def whole(array):
    return pl.BlockSpec(array.shape, lambda *_: (0,) * array.ndim)


def after(value, *others):
    anywhere = pl.BlockSpec(memory_space=pl.ANY)
    return pl.pallas_call(
        lambda *refs: None,
        in_specs=[anywhere] * (1 + len(others)),
        out_specs=anywhere,
        out_shape=jax.ShapeDtypeStruct(value.shape, value.dtype),
        input_output_aliases={0: 0},
        compiler_params=pltpu.CompilerParams(vmem_limit_bytes=MIB),
        cost_estimate=pl.CostEstimate(flops=0, bytes_accessed=0, transcendentals=0),
        name="after",
    )(value, *others)


def tables_kernel(
    leaf_ref, weights_ref, mine_ref, theirs_ref, shifted_ref, inverse_ref, message_ref, left_ref, right_ref
):
    child = pl.program_id(0)
    table = log_softmax_by_value(leaf_ref[0])
    peak = jnp.max(table, axis=1, keepdims=True)
    shifted = jnp.exp(table - peak).astype(BF16)
    shifted_ref[0] = shifted
    totals = dot_t(shifted, weights_ref[0])
    inverse_ref[0] = (1.0 / totals).astype(BF16)
    message = (peak + jnp.log(totals)).astype(BF16)
    message_ref[0] = message
    values = message.shape[0]
    rows = pl.ds(pl.multiple_of(child * values, values), values)
    part = left_ref.shape[1]
    left_ref[rows] = message[:, :part]
    right_ref[rows] = message[:, part:]

    @pl.when(child == 0)
    def _():
        children = mine_ref.shape[0]
        core = lax.axis_index("batch")
        mine, theirs = mine_ref[...], theirs_ref[...]
        low, high = jnp.where(core == 0, mine, theirs), jnp.where(core == 0, theirs, mine)
        filler = jnp.zeros((16 - 2 * children, mine.shape[1]), F32)
        rows = jnp.concatenate([low.astype(F32), high.astype(F32), filler])
        left_ref[left_ref.shape[0] - 16 :] = rows.astype(BF16)


def tables(leaf, weights, mine, theirs):
    children, states, values = leaf.shape
    one = lambda *block: pl.BlockSpec((1, *block), lambda c: (c, 0, 0))
    left = shape(children * values + 16, states // 2)
    right = shape(children * values, states // 2)
    return call(
        tables_kernel, "tables", (children,),
        [one(states, values), one(states, states), whole(mine), whole(theirs)],
        [one(values, states)] * 3 + [whole(left), whole(right)],
        [shape(children, values, states)] * 3 + [left, right],
        (leaf, weights, mine, theirs),
        2 * children * values * states**2,
        scalars=0,
    )


def rows_kernel(
    ids_ref, parent_pix_ref, pix_ref, leaf_ref, message_ref, shifted_ref, inverse_ref,
    shifted_rows_ref, inverse_rows_ref, out_ref, token_ref,
):
    token_ref[...] = jnp.zeros_like(token_ref)
    child, children = pl.program_id(0), pix_ref.shape[0]
    position = lax.axis_index("region")
    values = message_ref.shape[1]
    hot = one_hot(pix_ref[pl.ds(child, 1)], values)
    shifted_rows_ref[0] = dot(hot, shifted_ref[0]).astype(BF16)
    inverse_rows_ref[0] = dot(hot, inverse_ref[0]).astype(BF16)
    mine = jnp.where(ids_ref[position * children + child] == position, 1.0, 0.0)
    message = dot(hot, message_ref[0]) * mine

    @pl.when(child == 0)
    def _():
        logits = leaf_ref[0]
        wide = logits.astype(F32)
        top = jnp.max(wide, axis=1, keepdims=True)
        norm = top + jnp.log(jnp.sum(jnp.exp(wide - top), axis=1, keepdims=True))
        norm_row = jnp.transpose(jnp.broadcast_to(norm, (norm.shape[0], 128)))[:1]
        parent_hot = one_hot(parent_pix_ref[...], values)
        out_ref[0] = dot_t(parent_hot, logits) - norm_row + message

    @pl.when(child > 0)
    def _():
        out_ref[0] += message


def rows(ids, parent_pix, pix, leaf, message, shifted, inverse):
    children, values, states = message.shape
    samples = pix.shape[1]
    one = lambda *block: pl.BlockSpec((1, *block), lambda c, ids: (c, 0, 0))
    out = shape(1, samples, states, dtype=F32)
    return call(
        rows_kernel, "rows", (children,),
        [whole(parent_pix), whole(pix), whole(leaf)] + [one(values, states)] * 3,
        [one(samples, states)] * 2 + [whole(out), whole(TOKEN)],
        [shape(children, samples, states)] * 2 + [out, TOKEN],
        (ids, parent_pix, pix, leaf, message, shifted, inverse),
        2 * samples * states * values * (3 * children + 1),
    )


def sums_kernel(
    ids_ref, pix_ref, first_ref, here_ref, second_ref, inverse_ref, scaled_ref, mine_ref, theirs_ref
):
    child, children = pl.program_id(0), pl.num_programs(0)
    position, core = lax.axis_index("region"), lax.axis_index("batch")
    source = ids_ref[position * children + child] - position
    in_first = (source < 0) == (core == 0)
    above = jnp.where(source == 0, here_ref[0], jnp.where(in_first, first_ref[0], second_ref[0]))
    values, part = mine_ref.shape[1:]
    hot_rows = one_hot_rows(pix_ref[pl.ds(child, 1)], values).astype(BF16)
    sums = dot(hot_rows, above)
    low, high = sums[:, :part], sums[:, part:]
    mine_ref[0] = jnp.where(core == 0, low, high)
    theirs_ref[0] = jnp.where(core == 0, high, low).astype(BF16)
    scaled_ref[0] = (above.astype(F32) * inverse_ref[0].astype(F32)).astype(BF16)


def sums(ids, pix, first, here, second, inverse, values):
    children, samples, states = inverse.shape
    one = lambda *block: pl.BlockSpec((1, *block), lambda c, ids: (c, 0, 0))
    return call(
        sums_kernel, "sums", (children,),
        [whole(pix), whole(first), whole(here), whole(second), one(samples, states)],
        [one(samples, states), one(values, states // 2), one(values, states // 2)],
        [
            shape(children, samples, states),
            shape(children, values, states // 2, dtype=F32),
            shape(children, values, states // 2),
        ],
        (ids, pix, first, here, second, inverse),
        5 * 10**16,
        vmem=24,
    )


def flows_kernel(scaled_ref, shifted_ref, weights_ref, flows_ref, token_ref):
    token_ref[...] = jnp.zeros_like(token_ref)
    pulled = dot(scaled_ref[0], weights_ref[0])
    flows_ref[0] = (shifted_ref[0].astype(F32) * pulled).astype(BF16)


def flows(scaled, shifted, weights):
    children, samples, states = shifted.shape
    one = lambda *block: pl.BlockSpec((1, *block), lambda c: (c, 0, 0))
    return call(
        flows_kernel, "flows", (children,),
        [one(samples, states)] * 2 + [one(states, states)],
        [one(samples, states), whole(TOKEN)],
        [shape(children, samples, states), TOKEN],
        (scaled, shifted, weights),
        5 * 10**16,
        vmem=24,
        scalars=0,
    )


def update_kernel(
    mine_ref, theirs_ref, inverse_ref, shifted_ref, weights_ref, _, out_ref, token_ref, held_ref, sems
):
    child = pl.program_id(0)
    children, count, _ = held_ref.shape
    start = pl.multiple_of(lax.axis_index("batch") * count, count)
    token_ref[...] = jnp.zeros_like(token_ref)

    def fetch(c):
        return pltpu.make_async_copy(
            weights_ref.at[c, pl.ds(start, count)], held_ref.at[c], sems.at[c]
        )

    @pl.when(child == 0)
    def _():
        for c in range(children):
            fetch(c).start()

    inverse = inverse_ref[0, :, pl.ds(start, count)]
    sums = (mine_ref[0] + theirs_ref[0].astype(F32)) * inverse.astype(F32)
    scaled = jnp.transpose(sums).astype(BF16)
    fetch(child).wait()
    width = STRIP
    for at in range(0, count, width):
        pairs = dot(scaled[at : at + width], shifted_ref[0])
        counts = held_ref[child, at : at + width].astype(F32) * pairs + PRIOR
        scale = counts.shape[1] / jnp.sum(counts, axis=1, keepdims=True)
        out_ref[0, at : at + width] = (counts * scale).astype(BF16)


def update(mine, theirs, inverse, shifted, weights, ready):
    children, values, states = shifted.shape
    count = mine.shape[2]
    one = lambda *block: pl.BlockSpec((1, *block), lambda c: (c, 0, 0))
    return call(
        update_kernel, "update", (children,),
        [one(values, count)] * 2 + [one(values, states)] * 2 + [pl.BlockSpec(memory_space=pltpu.HBM), whole(TOKEN)],
        [one(count, states), whole(TOKEN)],
        [shape(children, count, states), TOKEN],
        (mine, theirs, inverse, shifted, weights, ready),
        2 * children * count * states * values,
        vmem=26,
        scalars=0,
        scratch=[pltpu.VMEM((children, count, states), BF16), pltpu.SemaphoreType.DMA((children,))],
    )


def add_messages(children, landed, ids_ref, table_ref, hot_ref, sum_ref, pixels=False):
    count, values = ids_ref.shape[0], hot_ref.shape[2]
    position, core = lax.axis_index("region"), lax.axis_index("batch")
    neighbour = jnp.where((core == 0) == landed, position - 1, position + 1)
    for c in range(children):
        child = neighbour * children + c
        there = jnp.logical_and(child >= 0, child < count)
        parent = ids_ref[jnp.clip(child, 0, count - 1)]

        @pl.when(jnp.logical_and(there, parent == position))
        def _():
            if pixels:
                halves = table_ref[children * values :].astype(F32)
                low, high = halves[c : c + 1], halves[children + c : children + c + 1]
                hot_ref[c] = one_hot(jnp.where(core == 0, low, high), values)
            sum_ref[...] += dot(hot_ref[c], table_ref[c * values : (c + 1) * values])


def first_kernel(children, ids_ref, left_ref, near_ref, sum_ref, hot_ref, token_ref):
    token_ref[...] = jnp.zeros_like(token_ref)
    sum_ref[...] = near_ref[0, :, : sum_ref.shape[1]]
    add_messages(children, True, ids_ref, left_ref, hot_ref, sum_ref, pixels=True)


def write(total_ref, out_ref, start, sem):
    columns = pl.ds(start, total_ref.shape[1])
    return pltpu.make_async_copy(total_ref, out_ref.at[0, :, columns], sem)


def middle_kernel(
    children, ids_ref, left_ref, right_ref, near_ref, sum_ref, hot_ref,
    out_ref, next_ref, other_hot_ref, total_ref, sem,
):
    total_ref[...] = sum_ref[...]
    add_messages(children, False, ids_ref, left_ref, other_hot_ref, total_ref, pixels=True)
    copy = write(total_ref, out_ref, 0, sem)
    copy.start()
    next_ref[...] = near_ref[0, :, next_ref.shape[1] :]
    add_messages(children, True, ids_ref, right_ref, hot_ref, next_ref)
    copy.wait()


def last_kernel(children, ids_ref, right_ref, sum_ref, hot_ref, _, out_ref, low_ref, high_ref, sems):
    part = low_ref.shape[1]
    copies = []
    for i, total_ref in enumerate((low_ref, high_ref)):
        columns = pl.ds(i * part, part)
        total_ref[...] = sum_ref[:, columns]
        add_messages(children, False, ids_ref, right_ref.at[:, columns], hot_ref, total_ref)
        copies.append(write(total_ref, out_ref, (2 + i) * part, sems.at[i]))
        copies[i].start()
    for copy in copies:
        copy.wait()


def gather(kernel, name, children, args, out_specs, out_shape, anywhere=(), **more):
    in_specs = [pl.BlockSpec(memory_space=pltpu.VMEM)] * (len(args) - 1 - len(anywhere))
    return call(
        functools.partial(kernel, children), name, (1,),
        in_specs + [pl.BlockSpec(memory_space=pl.ANY)] * len(anywhere),
        out_specs, out_shape, args, 10**9, vmem=20, **more,
    )


def on_device(
    child_pixels, parent_pixels, child_leaf, parent_leaf, edge_weights, parent_of, parent_flows
):
    regions, cores = lax.axis_size("region"), lax.axis_size("batch")
    rows_of = lambda core, step: [
        (cores * i + core, cores * (i + step) + core)
        for i in range(regions)
        if 0 <= i + step < regions
    ]
    out_first = rows_of(0, 1) + rows_of(1, -1)
    out_second = rows_of(1, 1) + rows_of(0, -1)
    swap = [(0, 1), (1, 0)]
    children, values = child_pixels.shape[0], child_leaf.shape[2]

    first = lax.ppermute(parent_flows, ("region", "batch"), out_first)
    second = lax.ppermute(parent_flows, ("region", "batch"), out_second)
    other_pix = lax.ppermute(child_pixels, "batch", swap)
    shifted, inverse, message, left, right = tables(child_leaf, edge_weights, child_pixels, other_pix)
    shifted_rows, inverse_rows, near, looked_up = rows(
        parent_of, parent_pixels, child_pixels, parent_leaf, message, shifted, inverse
    )
    left = after(left, looked_up)
    right = lax.ppermute(after(right, left), ("region", "batch"), out_first)
    left = lax.ppermute(left, ("region", "batch"), out_first)
    scaled, mine, theirs = sums(
        parent_of, child_pixels, first, parent_flows, second, inverse_rows, values
    )
    theirs = lax.ppermute(theirs, "batch", swap)
    child_flows, flowed = flows(scaled, shifted_rows, edge_weights)
    new_weights, updated = update(mine, theirs, inverse, shifted, edge_weights, flowed)
    left = after(left, updated)
    other_left = lax.ppermute(left, "batch", swap)
    samples, states = near.shape[1:]
    in_vmem, in_hbm = pl.BlockSpec(memory_space=pltpu.VMEM), pl.BlockSpec(memory_space=pl.ANY)
    full, part = shape(*near.shape, dtype=F32), shape(samples, states // 2, dtype=F32)
    hot_shape = shape(children, samples, values)
    total, hot, started = gather(
        first_kernel, "first", children, (parent_of, left, near),
        [in_vmem] * 3, [part, hot_shape, TOKEN],
    )
    right = after(right, started)
    other_right = lax.ppermute(right, "batch", swap)
    parent_ll, total, hot = gather(
        middle_kernel, "middle", children, (parent_of, other_left, right, near, total, hot),
        [in_hbm, in_vmem, in_vmem], [full, part, hot_shape],
        scratch=[pltpu.VMEM((samples, states // 2), F32), pltpu.SemaphoreType.DMA],
    )
    parent_ll = gather(
        last_kernel, "last", children, (parent_of, other_right, total, hot, parent_ll),
        in_hbm, full, anywhere=(parent_ll,), input_output_aliases={4: 0},
        scratch=[pltpu.VMEM((samples, states // 4), F32)] * 2 + [pltpu.SemaphoreType.DMA((2,))],
    )
    return parent_ll, child_flows, new_weights


def solution(mesh):
    return jax.shard_map(
        on_device,
        mesh=mesh,
        in_specs=(
            P("region", "batch"),
            P("region", "batch"),
            P("region", None, None),
            P("region", None, None),
            P("region", None, None),
            P(),
            P("region", "batch", None),
        ),
        out_specs=(
            P("region", "batch", None),
            P("region", "batch", None),
            P("region", "batch", None),
        ),
        check_vma=False,
    )
```

profile of v0, /device:TPU:5, one launch (start us, length us, event | category | flops | bytes accessed | tf_op | source)
XLA Modules:
  0.0 51.7 jit_solution(5232937872727235131)
XLA Ops:
  0.6 9.9 %collective-permute-start.3 = (bf16[1,512,1024]{2,1,0:T(8,128)(2,1)}, bf16[1,512,1024]{2,1,0:T(8,128)(2,1)S(1)}, u32[]{:S(2)}, u32[]{:S(2)}) collective-permute-start(bf16[1,512,1024]{2,1,0:T(8,128)(2,1)} %here_ref.1), channel_id=1, source_target_pairs={{0,2},{2,4},{4,6},{6,8},{8,10},{10,12},{12,14},{14,16},{16,18},{18... | collective-permute-start | bytes 3145736 | tf_op jit(solution)/shard_map/ppermute | solution.py:356
  10.5 1.9 %collective-permute-start.4 = (bf16[1,512,1024]{2,1,0:T(8,128)(2,1)}, bf16[1,512,1024]{2,1,0:T(8,128)(2,1)S(1)}, u32[]{:S(2)}, u32[]{:S(2)}) collective-permute-start(bf16[1,512,1024]{2,1,0:T(8,128)(2,1)} %here_ref.1), channel_id=1, source_target_pairs={{1,3},{3,5},{5,7},{7,9},{9,11},{11,13},{13,15},{15,17},{17,19},{19... | collective-permute-start | bytes 3145736 | tf_op jit(solution)/shard_map/ppermute | solution.py:357
  12.5 1.0 %collective-permute-start = (s32[2,512]{1,0:T(2,128)}, s32[2,512]{1,0:T(2,128)S(1)}, u32[]{:S(2)}, u32[]{:S(2)}) collective-permute-start(s32[2,512]{1,0:T(2,128)} %pix_ref.3), channel_id=1, source_target_pairs={{0,1},{1,0},{2,3},{3,2},{4,5},{5,4},{6,7},{7,6},{8,9},{9,8},{10,11... | collective-permute-start | bytes 12296 | tf_op jit(solution)/shard_map/ppermute | solution.py:358
  13.5 1.0 %collective-permute-done.theirs_ref = s32[2,512]{1,0:T(2,128)S(1)} collective-permute-done((s32[2,512]{1,0:T(2,128)}, s32[2,512]{1,0:T(2,128)S(1)}, u32[]{:S(2)}, u32[]{:S(2)}) %collective-permute-start) | collective-permute-done | bytes 4128 | tf_op jit(solution)/shard_map/ppermute | solution.py:358
  14.6 2.2 %copy-done = bf16[2,1024,1024]{2,1,0:T(8,128)(2,1)S(1)} copy-done((bf16[2,1024,1024]{2,1,0:T(8,128)(2,1)S(1)}, bf16[2,1024,1024]{2,1,0:T(8,128)(2,1)}, u32[]{:S(2)}) %copy-start) | copy-done | bytes 4194328
  16.7 1.2 %copy-done.2 = bf16[2,1024,256]{2,1,0:T(8,128)(2,1)S(1)} copy-done((bf16[2,1024,256]{2,1,0:T(8,128)(2,1)S(1)}, bf16[2,1024,256]{2,1,0:T(8,128)(2,1)}, u32[]{:S(2)}) %copy-start.2) | copy-done | bytes 1048600
  18.0 0.7 %copy-done.4 = s32[2,512]{1,0:T(2,128)S(1)} copy-done((s32[2,512]{1,0:T(2,128)S(1)}, s32[2,512]{1,0:T(2,128)}, u32[]{:S(2)}) %copy-start.4) | copy-done | bytes 4120
  18.7 2.8 %tables.1 = (bf16[2,256,1024]{2,1,0:T(8,128)(2,1)S(1)}, bf16[2,256,1024]{2,1,0:T(8,128)(2,1)S(1)}, bf16[2,256,1024]{2,1,0:T(8,128)(2,1)S(1)}, bf16[528,512]{1,0:T(8,128)(2,1)S(1)}, bf16[512,512]{1,0:T(8,128)(2,1)S(1)}) custom-call(bf16[2,1024,256]{2,1,0:T(8,128)(2,1)S(1)} %copy-done.2, bf16[2,1024,1024]{2,1,0:T(8,128)(2,1)S(1)} %copy-done, ...), custom_call_target="tpu_custom_call" | custom-call | flops 1073 | bytes 8 | tf_op jit(solution)/shard_map/tables/pallas_call | solution.py:44
  21.4 0.0 copy-done.3
  21.5 0.0 copy-done.5
  21.5 4.6 %rows.1 = (bf16[2,512,1024]{2,1,0:T(8,128)(2,1)S(1)}, bf16[2,512,1024]{2,1,0:T(8,128)(2,1)S(1)}, f32[1,512,1024]{2,1,0:T(8,128)S(1)}, f32[8,128]{1,0:T(8,128)S(1)}) custom-call(s32[256]{0:T(256)S(1)} %copy-done.6, s32[1,512]{1,0:T(1,128)S(1)} %copy-done.7, s32[2,512]{1,0:T(2,128)S(1)} %copy-done.5, bf16[1,1024,256]{2,1,0:T(8,128)(2,1)S(1)} %copy-done.3, ...), custom_call_target="tpu_custom_call" | custom-call | flops 1879 | bytes 8 | tf_op jit(solution)/shard_map/rows/pallas_call | solution.py:44
  26.1 0.0 copy-start.8
  26.1 7.1 %collective-permute-start.2 = (bf16[528,512]{1,0:T(8,128)(2,1)S(1)}, bf16[528,512]{1,0:T(8,128)(2,1)S(1)}, u32[]{:S(2)}, u32[]{:S(2)}) collective-permute-start(bf16[528,512]{1,0:T(8,128)(2,1)S(1)} %after.4.refs_1_), channel_id=1, source_target_pairs={{0,2},{2,4},{4,6},{6,8},{8,10},{10,12},{12,14},{14,16},{16,18},{18... | collective-permute-start | bytes 1622024 | tf_op jit(solution)/shard_map/ppermute | solution.py:365
  33.2 1.9 %collective-permute-start.1 = (bf16[512,512]{1,0:T(8,128)(2,1)S(1)}, bf16[512,512]{1,0:T(8,128)(2,1)S(1)}, u32[]{:S(2)}, u32[]{:S(2)}) collective-permute-start(bf16[512,512]{1,0:T(8,128)(2,1)S(1)} %after.5), channel_id=1, source_target_pairs={{0,2},{2,4},{4,6},{6,8},{8,10},{10,12},{12,14},{14,16},{16,18},{18... | collective-permute-start | bytes 1572872 | tf_op jit(solution)/shard_map/ppermute | solution.py:364
  35.1 0.0 collective-permute-done.3.first_ref
  35.1 0.0 collective-permute-done.4.second_ref
  35.1 0.0 copy-start.1
  35.2 1.9 %sums.1 = (bf16[2,512,1024]{2,1,0:T(8,128)(2,1)S(1)}, f32[2,256,512]{2,1,0:T(8,128)S(1)}, bf16[2,256,512]{2,1,0:T(8,128)(2,1)S(1)}) custom-call(s32[256]{0:T(256)S(1)} %copy-done.6, s32[2,512]{1,0:T(2,128)S(1)} %copy-done.5, bf16[1,512,1024]{2,1,0:T(8,128)(2,1)S(1)} %collective-permute-done.3.first_ref, bf16[1,512,1024]{2,1,0:T(8,128)(2,1)S(1)} %copy-done.8, ...), custom_call_target="tpu_custom_call" | custom-call | flops 49999998976 | bytes 8 | tf_op jit(solution)/shard_map/sums/pallas_call | solution.py:44
  37.0 0.1 collective-permute-start.5
  37.1 0.2 copy-done.1
  37.3 3.5 %flows.1 = (bf16[2,512,1024]{2,1,0:T(8,128)(2,1)}, f32[8,128]{1,0:T(8,128)S(1)}) custom-call(bf16[2,512,1024]{2,1,0:T(8,128)(2,1)S(1)} %get-tuple-element.34.scaled_ref, bf16[2,512,1024]{2,1,0:T(8,128)(2,1)S(1)} %get-tuple-element.35.shifted_ref, bf16[2,1024,1024]{2,1,0:T(8,128)(2,1)S(1)} %copy-done.1), custom_call_target="tpu_custom_call" | custom-call | flops 49999998976 | bytes 8 | tf_op jit(solution)/shard_map/flows/pallas_call | solution.py:44
  40.9 0.0 collective-permute-done.5.theirs_ref
  40.9 3.1 %update.1 = (bf16[2,512,1024]{2,1,0:T(8,128)(2,1)}, f32[8,128]{1,0:T(8,128)S(1)}) custom-call(f32[2,256,512]{2,1,0:T(8,128)S(1)} %get-tuple-element.32.mine_ref, bf16[2,256,512]{2,1,0:T(8,128)(2,1)S(1)} %collective-permute-done.5.theirs_ref, bf16[2,256,1024]{2,1,0:T(8,128)(2,1)S(1)} %get-tuple-element.29.inverse_ref, ...), custom_call_target="tpu_custom_call" | custom-call | flops 536 | bytes 8 | tf_op jit(solution)/shard_map/update/pallas_call | solution.py:44
  44.0 0.0 collective-permute-done.2.refs_0_
  44.0 0.4 collective-permute-start.7
  44.4 0.6 %first.1 = (f32[512,512]{1,0:T(8,128)S(1)}, bf16[2,512,256]{2,1,0:T(8,128)(2,1)S(1)}, f32[8,128]{1,0:T(8,128)S(1)}) custom-call(s32[256]{0:T(256)S(1)} %copy-done.6, bf16[528,512]{1,0:T(8,128)(2,1)S(1)} %after.6.left_ref, f32[1,512,1024]{2,1,0:T(8,128)S(1)} %get-tuple-element.38.near_ref), custom_call_target="tpu_custom_call" | custom-call | flops 1000 | bytes 8 | tf_op jit(solution)/shard_map/first/pallas_call | solution.py:44
  45.0 0.1 collective-permute-done.1.refs_0_
  45.1 2.5 %collective-permute-start.6 = (bf16[512,512]{1,0:T(8,128)(2,1)S(1)}, bf16[512,512]{1,0:T(8,128)(2,1)S(1)}, u32[]{:S(2)}, u32[]{:S(2)}) collective-permute-start(bf16[512,512]{1,0:T(8,128)(2,1)S(1)} %after.7.right_ref), channel_id=1, source_target_pairs={{0,1},{1,0},{2,3},{3,2},{4,5},{5,4},{6,7},{7,6},{8,9},{9,8},{10,11... | collective-permute-start | bytes 1572872 | tf_op jit(solution)/shard_map/ppermute | solution.py:383
  47.6 0.0 collective-permute-done.7.left_ref
  47.6 2.2 %middle.1 = (f32[1,512,1024]{2,1,0:T(8,128)}, f32[512,512]{1,0:T(8,128)S(1)}, bf16[2,512,256]{2,1,0:T(8,128)(2,1)S(1)}) custom-call(s32[256]{0:T(256)S(1)} %copy-done.6, bf16[528,512]{1,0:T(8,128)(2,1)S(1)} %collective-permute-done.7.left_ref, bf16[512,512]{1,0:T(8,128)(2,1)S(1)} %after.7.right_ref, f32[1,512,1024]{2,1,0:T(8,128)S(1)} %get-tuple-element.38.near_ref, ...), custom_call_target="tpu_custom_call" | custom-call | flops 1000 | bytes 8 | tf_op jit(solution)/shard_map/middle/pallas_call | solution.py:44
  49.8 0.0 collective-permute-done.6.right_ref
  49.8 1.9 %last.1 = f32[1,512,1024]{2,1,0:T(8,128)} custom-call(s32[256]{0:T(256)S(1)} %copy-done.6, bf16[512,512]{1,0:T(8,128)(2,1)S(1)} %collective-permute-done.6.right_ref, f32[512,512]{1,0:T(8,128)S(1)} %get-tuple-element.42.sum_ref, bf16[2,512,256]{2,1,0:T(8,128)(2,1)S(1)} %get-tuple-element.43.hot_ref, ...), custom_call_target="tpu_custom_call", output_to_operand_aliasing={{}: (4, {})} | custom-call | flops 1000 | bytes 8 | tf_op jit(solution)/shard_map/last/pallas_call | solution.py:44
  (14 shorter events, 0.0 us)
Async XLA Ops:
  0.6 34.5 %collective-permute-start.3 = (bf16[1,512,1024]{2,1,0:T(8,128)(2,1)}, bf16[1,512,1024]{2,1,0:T(8,128)(2,1)S(1)}, u32[]{:S(2)}, u32[]{:S(2)}) collective-permute-start(bf16[1,512,1024]{2,1,0:T(8,128)(2,1)} %here_ref.1), channel_id=1, source_target_pairs={{0,2},{2,4},{4,6},{6,8},{8,10},{10,12},{12,14},{14,16},{16,18},{18... | collective-permute-start | bytes 3145736 | tf_op jit(solution)/shard_map/ppermute | solution.py:356
  10.5 24.6 %collective-permute-start.4 = (bf16[1,512,1024]{2,1,0:T(8,128)(2,1)}, bf16[1,512,1024]{2,1,0:T(8,128)(2,1)S(1)}, u32[]{:S(2)}, u32[]{:S(2)}) collective-permute-start(bf16[1,512,1024]{2,1,0:T(8,128)(2,1)} %here_ref.1), channel_id=1, source_target_pairs={{1,3},{3,5},{5,7},{7,9},{9,11},{11,13},{13,15},{15,17},{17,19},{19... | collective-permute-start | bytes 3145736 | tf_op jit(solution)/shard_map/ppermute | solution.py:357
  12.5 2.1 %collective-permute-start = (s32[2,512]{1,0:T(2,128)}, s32[2,512]{1,0:T(2,128)S(1)}, u32[]{:S(2)}, u32[]{:S(2)}) collective-permute-start(s32[2,512]{1,0:T(2,128)} %pix_ref.3), channel_id=1, source_target_pairs={{0,1},{1,0},{2,3},{3,2},{4,5},{5,4},{6,7},{7,6},{8,9},{9,8},{10,11... | collective-permute-start | bytes 12296 | tf_op jit(solution)/shard_map/ppermute | solution.py:358
  14.6 2.2 %copy-start = (bf16[2,1024,1024]{2,1,0:T(8,128)(2,1)S(1)}, bf16[2,1024,1024]{2,1,0:T(8,128)(2,1)}, u32[]{:S(2)}) copy-start(bf16[2,1024,1024]{2,1,0:T(8,128)(2,1)} %weights_ref.5) | copy-start | bytes 12582916
  16.7 1.2 %copy-start.2 = (bf16[2,1024,256]{2,1,0:T(8,128)(2,1)S(1)}, bf16[2,1024,256]{2,1,0:T(8,128)(2,1)}, u32[]{:S(2)}) copy-start(bf16[2,1024,256]{2,1,0:T(8,128)(2,1)} %leaf_ref.2) | copy-start | bytes 3145732
  18.0 0.7 %copy-start.4 = (s32[2,512]{1,0:T(2,128)S(1)}, s32[2,512]{1,0:T(2,128)}, u32[]{:S(2)}) copy-start(s32[2,512]{1,0:T(2,128)} %pix_ref.3) | copy-start | bytes 12292
  18.7 2.8 %copy-start.3 = (bf16[1,1024,256]{2,1,0:T(8,128)(2,1)S(1)}, bf16[1,1024,256]{2,1,0:T(8,128)(2,1)}, u32[]{:S(2)}) copy-start(bf16[1,1024,256]{2,1,0:T(8,128)(2,1)} %leaf_ref.3) | copy-start | bytes 1572868
  18.7 2.8 %copy-start.5 = (s32[2,512]{1,0:T(2,128)S(1)}, s32[2,512]{1,0:T(2,128)}, u32[]{:S(2)}) copy-start(s32[2,512]{1,0:T(2,128)} %pix_ref.3) | copy-start | bytes 12292
  18.7 2.8 %copy-start.6 = (s32[256]{0:T(256)S(1)}, s32[256]{0:T(256)}, u32[]{:S(2)}) copy-start(s32[256]{0:T(256)} %ids_ref.9) | copy-start | bytes 3076
  18.7 2.8 %copy-start.7 = (s32[1,512]{1,0:T(1,128)S(1)}, s32[1,512]{1,0:T(1,128)}, u32[]{:S(2)}) copy-start(s32[1,512]{1,0:T(1,128)} %parent_pix_ref.1) | copy-start | bytes 6148
  26.1 9.1 %copy-start.8 = (bf16[1,512,1024]{2,1,0:T(8,128)(2,1)S(1)}, bf16[1,512,1024]{2,1,0:T(8,128)(2,1)}, u32[]{:S(2)}) copy-start(bf16[1,512,1024]{2,1,0:T(8,128)(2,1)} %here_ref.1) | copy-start | bytes 3145732
  26.1 17.9 %collective-permute-start.2 = (bf16[528,512]{1,0:T(8,128)(2,1)S(1)}, bf16[528,512]{1,0:T(8,128)(2,1)S(1)}, u32[]{:S(2)}, u32[]{:S(2)}) collective-permute-start(bf16[528,512]{1,0:T(8,128)(2,1)S(1)} %after.4.refs_1_), channel_id=1, source_target_pairs={{0,2},{2,4},{4,6},{6,8},{8,10},{10,12},{12,14},{14,16},{16,18},{18... | collective-permute-start | bytes 1622024 | tf_op jit(solution)/shard_map/ppermute | solution.py:365
  33.2 11.9 %collective-permute-start.1 = (bf16[512,512]{1,0:T(8,128)(2,1)S(1)}, bf16[512,512]{1,0:T(8,128)(2,1)S(1)}, u32[]{:S(2)}, u32[]{:S(2)}) collective-permute-start(bf16[512,512]{1,0:T(8,128)(2,1)S(1)} %after.5), channel_id=1, source_target_pairs={{0,2},{2,4},{4,6},{6,8},{8,10},{10,12},{12,14},{14,16},{16,18},{18... | collective-permute-start | bytes 1572872 | tf_op jit(solution)/shard_map/ppermute | solution.py:364
  35.1 2.2 %copy-start.1 = (bf16[2,1024,1024]{2,1,0:T(8,128)(2,1)S(1)}, bf16[2,1024,1024]{2,1,0:T(8,128)(2,1)}, u32[]{:S(2)}) copy-start(bf16[2,1024,1024]{2,1,0:T(8,128)(2,1)} %weights_ref.5) | copy-start | bytes 12582916
  37.0 3.8 %collective-permute-start.5 = (bf16[2,256,512]{2,1,0:T(8,128)(2,1)S(1)}, bf16[2,256,512]{2,1,0:T(8,128)(2,1)S(1)}, u32[]{:S(2)}, u32[]{:S(2)}) collective-permute-start(bf16[2,256,512]{2,1,0:T(8,128)(2,1)S(1)} %get-tuple-element.33), channel_id=1, source_target_pairs={{0,1},{1,0},{2,3},{3,2},{4,5},{5,4},{6,7},{7,6},{8,9},{9,8},{10,11... | collective-permute-start | bytes 1572872 | tf_op jit(solution)/shard_map/ppermute | solution.py:369
  44.0 3.6 %collective-permute-start.7 = (bf16[528,512]{1,0:T(8,128)(2,1)S(1)}, bf16[528,512]{1,0:T(8,128)(2,1)S(1)}, u32[]{:S(2)}, u32[]{:S(2)}) collective-permute-start(bf16[528,512]{1,0:T(8,128)(2,1)S(1)} %after.6.left_ref), channel_id=1, source_target_pairs={{0,1},{1,0},{2,3},{3,2},{4,5},{5,4},{6,7},{7,6},{8,9},{9,8},{10,11... | collective-permute-start | bytes 1622024 | tf_op jit(solution)/shard_map/ppermute | solution.py:373
  45.1 4.7 %collective-permute-start.6 = (bf16[512,512]{1,0:T(8,128)(2,1)S(1)}, bf16[512,512]{1,0:T(8,128)(2,1)S(1)}, u32[]{:S(2)}, u32[]{:S(2)}) collective-permute-start(bf16[512,512]{1,0:T(8,128)(2,1)S(1)} %after.7.right_ref), channel_id=1, source_target_pairs={{0,1},{1,0},{2,3},{3,2},{4,5},{5,4},{6,7},{7,6},{8,9},{9,8},{10,11... | collective-permute-start | bytes 1572872 | tf_op jit(solution)/shard_map/ppermute | solution.py:383
where the time goes:
time: 52.4 us; the launch traced here: 51.7 us
  starting transfers between devices  24.8 us (47%)
  Pallas kernels  20.6 us (39%)
  local copies, waits for them, and re-layouts  4.32 us (8%)
  waiting for transfers between devices  1.17 us (2%)
  between operations  0.84 us (2%)
    pallas_call x8, Pallas kernels, call(): pl.pallas_call(kernel, grid_spec=pltpu.PrefetchScalarGridSpec(num_scalar_...  20.5 us
    ppermute x1, starting transfers between devices, on_device(): first = lax.ppermute(parent_flows, ('region', 'batch'), out_first)  9.91 us
    ppermute x1, starting transfers between devices, on_device(): left = lax.ppermute(left, ('region', 'batch'), out_first)  7.09 us
    unnamed x18, local copies, waits for them, and re-layouts  4.32 us
    ppermute x1, starting transfers between devices, on_device(): other_right = lax.ppermute(right, 'batch', swap)  2.5 us
    ppermute x1, starting transfers between devices, on_device(): second = lax.ppermute(parent_flows, ('region', 'batch'), out_second)  1.92 us
    ppermute x1, starting transfers between devices, on_device(): right = lax.ppermute(after(right, left), ('region', 'batch'), out_first)  1.92 us
  transfers between devices with their start and end apart: 8, of which 2 were waited for; matrix products, arithmetic and copies ran while one was open for 0% of the time, Pallas kernels for 36%

commit v1 on v0

--- a/solution.py
+++ b/solution.py
@@ -317,17 +317,12 @@
     copy.wait()
 
 
-def last_kernel(children, ids_ref, right_ref, sum_ref, hot_ref, _, out_ref, low_ref, high_ref, sems):
-    part = low_ref.shape[1]
-    copies = []
-    for i, total_ref in enumerate((low_ref, high_ref)):
-        columns = pl.ds(i * part, part)
-        total_ref[...] = sum_ref[:, columns]
-        add_messages(children, False, ids_ref, right_ref.at[:, columns], hot_ref, total_ref)
-        copies.append(write(total_ref, out_ref, (2 + i) * part, sems.at[i]))
-        copies[i].start()
-    for copy in copies:
-        copy.wait()
+def last_kernel(children, ids_ref, right_ref, sum_ref, hot_ref, _, out_ref, total_ref, sem):
+    total_ref[...] = sum_ref[...]
+    add_messages(children, False, ids_ref, right_ref, hot_ref, total_ref)
+    copy = write(total_ref, out_ref, total_ref.shape[1], sem)
+    copy.start()
+    copy.wait()
 
 
 def gather(kernel, name, children, args, out_specs, out_shape, anywhere=(), **more):
@@ -389,7 +384,7 @@
     parent_ll = gather(
         last_kernel, "last", children, (parent_of, other_right, total, hot, parent_ll),
         in_hbm, full, anywhere=(parent_ll,), input_output_aliases={4: 0},
-        scratch=[pltpu.VMEM((samples, states // 4), F32)] * 2 + [pltpu.SemaphoreType.DMA((2,))],
+        scratch=[pltpu.VMEM((samples, states // 2), F32), pltpu.SemaphoreType.DMA],
     )
     return parent_ll, child_flows, new_weights
 

time: 52.4 us -> 52.9 us (level)
  Pallas kernels: 20.6 us -> 22 us
    pallas_call x8, Pallas kernels: 20.5 us -> 22 us  [call(): pl.pallas_call(kernel, grid_spec=pltpu.PrefetchScalarGridSpec(num_scalar_...]
  transfers between devices with their start and end apart: 8 -> 8, of which waited for: 2 -> 1; matrix products, arithmetic and copies ran while one was open for 0% -> 0% of each run, Pallas kernels for 36% -> 38%
where the time goes in v1:
time: 52.9 us; the launch traced here: 52.6 us
  starting transfers between devices  24.4 us (46%)
  Pallas kernels  22 us (42%)
  local copies, waits for them, and re-layouts  4.32 us (8%)
  waiting for transfers between devices  1.05 us (2%)
  between operations  0.86 us (2%)
    pallas_call x8, Pallas kernels, call(): pl.pallas_call(kernel, grid_spec=pltpu.PrefetchScalarGridSpec(num_scalar_...  22 us
    ppermute x1, starting transfers between devices, on_device(): first = lax.ppermute(parent_flows, ('region', 'batch'), out_first)  9.91 us
    ppermute x1, starting transfers between devices, on_device(): left = lax.ppermute(left, ('region', 'batch'), out_first)  7.09 us
    unnamed x18, local copies, waits for them, and re-layouts  4.32 us
    ppermute x1, starting transfers between devices, on_device(): other_right = lax.ppermute(right, 'batch', swap)  2.04 us
    ppermute x1, starting transfers between devices, on_device(): second = lax.ppermute(parent_flows, ('region', 'batch'), out_second)  1.92 us
    ppermute x1, starting transfers between devices, on_device(): right = lax.ppermute(after(right, left), ('region', 'batch'), out_first)  1.92 us
  transfers between devices with their start and end apart: 8, of which 1 were waited for; matrix products, arithmetic and copies ran while one was open for 0% of the time, Pallas kernels for 38%

profile of v1, /device:TPU:5, one launch (start us, length us, event | category | flops | bytes accessed | tf_op | source)
XLA Modules:
  0.0 52.6 jit_solution(14917216181872845571)
XLA Ops:
  0.6 9.9 %collective-permute-start.3 = (bf16[1,512,1024]{2,1,0:T(8,128)(2,1)}, bf16[1,512,1024]{2,1,0:T(8,128)(2,1)S(1)}, u32[]{:S(2)}, u32[]{:S(2)}) collective-permute-start(bf16[1,512,1024]{2,1,0:T(8,128)(2,1)} %here_ref.1), channel_id=1, source_target_pairs={{0,2},{2,4},{4,6},{6,8},{8,10},{10,12},{12,14},{14,16},{16,18},{18... | collective-permute-start | bytes 3145736 | tf_op jit(solution)/shard_map/ppermute | solution.py:351
  10.5 1.9 %collective-permute-start.4 = (bf16[1,512,1024]{2,1,0:T(8,128)(2,1)}, bf16[1,512,1024]{2,1,0:T(8,128)(2,1)S(1)}, u32[]{:S(2)}, u32[]{:S(2)}) collective-permute-start(bf16[1,512,1024]{2,1,0:T(8,128)(2,1)} %here_ref.1), channel_id=1, source_target_pairs={{1,3},{3,5},{5,7},{7,9},{9,11},{11,13},{13,15},{15,17},{17,19},{19... | collective-permute-start | bytes 3145736 | tf_op jit(solution)/shard_map/ppermute | solution.py:352
  12.5 1.0 %collective-permute-start = (s32[2,512]{1,0:T(2,128)}, s32[2,512]{1,0:T(2,128)S(1)}, u32[]{:S(2)}, u32[]{:S(2)}) collective-permute-start(s32[2,512]{1,0:T(2,128)} %pix_ref.3), channel_id=1, source_target_pairs={{0,1},{1,0},{2,3},{3,2},{4,5},{5,4},{6,7},{7,6},{8,9},{9,8},{10,11... | collective-permute-start | bytes 12296 | tf_op jit(solution)/shard_map/ppermute | solution.py:353
  13.5 1.0 %collective-permute-done.theirs_ref = s32[2,512]{1,0:T(2,128)S(1)} collective-permute-done((s32[2,512]{1,0:T(2,128)}, s32[2,512]{1,0:T(2,128)S(1)}, u32[]{:S(2)}, u32[]{:S(2)}) %collective-permute-start) | collective-permute-done | bytes 4128 | tf_op jit(solution)/shard_map/ppermute | solution.py:353
  14.6 2.2 %copy-done = bf16[2,1024,1024]{2,1,0:T(8,128)(2,1)S(1)} copy-done((bf16[2,1024,1024]{2,1,0:T(8,128)(2,1)S(1)}, bf16[2,1024,1024]{2,1,0:T(8,128)(2,1)}, u32[]{:S(2)}) %copy-start) | copy-done | bytes 4194328
  16.7 1.2 %copy-done.2 = bf16[2,1024,256]{2,1,0:T(8,128)(2,1)S(1)} copy-done((bf16[2,1024,256]{2,1,0:T(8,128)(2,1)S(1)}, bf16[2,1024,256]{2,1,0:T(8,128)(2,1)}, u32[]{:S(2)}) %copy-start.2) | copy-done | bytes 1048600
  18.0 0.7 %copy-done.4 = s32[2,512]{1,0:T(2,128)S(1)} copy-done((s32[2,512]{1,0:T(2,128)S(1)}, s32[2,512]{1,0:T(2,128)}, u32[]{:S(2)}) %copy-start.4) | copy-done | bytes 4120
  18.7 2.8 %tables.1 = (bf16[2,256,1024]{2,1,0:T(8,128)(2,1)S(1)}, bf16[2,256,1024]{2,1,0:T(8,128)(2,1)S(1)}, bf16[2,256,1024]{2,1,0:T(8,128)(2,1)S(1)}, bf16[528,512]{1,0:T(8,128)(2,1)S(1)}, bf16[512,512]{1,0:T(8,128)(2,1)S(1)}) custom-call(bf16[2,1024,256]{2,1,0:T(8,128)(2,1)S(1)} %copy-done.2, bf16[2,1024,1024]{2,1,0:T(8,128)(2,1)S(1)} %copy-done, ...), custom_call_target="tpu_custom_call" | custom-call | flops 1073 | bytes 8 | tf_op jit(solution)/shard_map/tables/pallas_call | solution.py:44
  21.4 0.0 copy-done.3
  21.5 0.0 copy-done.5
  21.5 4.6 %rows.1 = (bf16[2,512,1024]{2,1,0:T(8,128)(2,1)S(1)}, bf16[2,512,1024]{2,1,0:T(8,128)(2,1)S(1)}, f32[1,512,1024]{2,1,0:T(8,128)S(1)}, f32[8,128]{1,0:T(8,128)S(1)}) custom-call(s32[256]{0:T(256)S(1)} %copy-done.6, s32[1,512]{1,0:T(1,128)S(1)} %copy-done.7, s32[2,512]{1,0:T(2,128)S(1)} %copy-done.5, bf16[1,1024,256]{2,1,0:T(8,128)(2,1)S(1)} %copy-done.3, ...), custom_call_target="tpu_custom_call" | custom-call | flops 1879 | bytes 8 | tf_op jit(solution)/shard_map/rows/pallas_call | solution.py:44
  26.1 0.0 copy-start.8
  26.1 7.1 %collective-permute-start.2 = (bf16[528,512]{1,0:T(8,128)(2,1)S(1)}, bf16[528,512]{1,0:T(8,128)(2,1)S(1)}, u32[]{:S(2)}, u32[]{:S(2)}) collective-permute-start(bf16[528,512]{1,0:T(8,128)(2,1)S(1)} %after.4.refs_1_), channel_id=1, source_target_pairs={{0,2},{2,4},{4,6},{6,8},{8,10},{10,12},{12,14},{14,16},{16,18},{18... | collective-permute-start | bytes 1622024 | tf_op jit(solution)/shard_map/ppermute | solution.py:360
  33.2 1.9 %collective-permute-start.1 = (bf16[512,512]{1,0:T(8,128)(2,1)S(1)}, bf16[512,512]{1,0:T(8,128)(2,1)S(1)}, u32[]{:S(2)}, u32[]{:S(2)}) collective-permute-start(bf16[512,512]{1,0:T(8,128)(2,1)S(1)} %after.5), channel_id=1, source_target_pairs={{0,2},{2,4},{4,6},{6,8},{8,10},{10,12},{12,14},{14,16},{16,18},{18... | collective-permute-start | bytes 1572872 | tf_op jit(solution)/shard_map/ppermute | solution.py:359
  35.1 0.0 collective-permute-done.3.first_ref
  35.1 0.0 collective-permute-done.4.second_ref
  35.1 0.0 copy-start.1
  35.2 1.9 %sums.1 = (bf16[2,512,1024]{2,1,0:T(8,128)(2,1)S(1)}, f32[2,256,512]{2,1,0:T(8,128)S(1)}, bf16[2,256,512]{2,1,0:T(8,128)(2,1)S(1)}) custom-call(s32[256]{0:T(256)S(1)} %copy-done.6, s32[2,512]{1,0:T(2,128)S(1)} %copy-done.5, bf16[1,512,1024]{2,1,0:T(8,128)(2,1)S(1)} %collective-permute-done.3.first_ref, bf16[1,512,1024]{2,1,0:T(8,128)(2,1)S(1)} %copy-done.8, ...), custom_call_target="tpu_custom_call" | custom-call | flops 49999998976 | bytes 8 | tf_op jit(solution)/shard_map/sums/pallas_call | solution.py:44
  37.0 0.1 collective-permute-start.5
  37.1 0.2 copy-done.1
  37.3 3.5 %flows.1 = (bf16[2,512,1024]{2,1,0:T(8,128)(2,1)}, f32[8,128]{1,0:T(8,128)S(1)}) custom-call(bf16[2,512,1024]{2,1,0:T(8,128)(2,1)S(1)} %get-tuple-element.34.scaled_ref, bf16[2,512,1024]{2,1,0:T(8,128)(2,1)S(1)} %get-tuple-element.35.shifted_ref, bf16[2,1024,1024]{2,1,0:T(8,128)(2,1)S(1)} %copy-done.1), custom_call_target="tpu_custom_call" | custom-call | flops 49999998976 | bytes 8 | tf_op jit(solution)/shard_map/flows/pallas_call | solution.py:44
  40.9 0.0 collective-permute-done.5.theirs_ref
  40.9 3.1 %update.1 = (bf16[2,512,1024]{2,1,0:T(8,128)(2,1)}, f32[8,128]{1,0:T(8,128)S(1)}) custom-call(f32[2,256,512]{2,1,0:T(8,128)S(1)} %get-tuple-element.32.mine_ref, bf16[2,256,512]{2,1,0:T(8,128)(2,1)S(1)} %collective-permute-done.5.theirs_ref, bf16[2,256,1024]{2,1,0:T(8,128)(2,1)S(1)} %get-tuple-element.29.inverse_ref, ...), custom_call_target="tpu_custom_call" | custom-call | flops 536 | bytes 8 | tf_op jit(solution)/shard_map/update/pallas_call | solution.py:44
  44.0 0.0 collective-permute-done.2.refs_0_
  44.0 0.4 collective-permute-start.7
  44.4 1.2 %first.1 = (f32[512,512]{1,0:T(8,128)S(1)}, bf16[2,512,256]{2,1,0:T(8,128)(2,1)S(1)}, f32[8,128]{1,0:T(8,128)S(1)}) custom-call(s32[256]{0:T(256)S(1)} %copy-done.6, bf16[528,512]{1,0:T(8,128)(2,1)S(1)} %after.6.left_ref, f32[1,512,1024]{2,1,0:T(8,128)S(1)} %get-tuple-element.38.near_ref), custom_call_target="tpu_custom_call" | custom-call | flops 1000 | bytes 8 | tf_op jit(solution)/shard_map/first/pallas_call | solution.py:44
  45.6 0.0 collective-permute-done.1.refs_0_
  45.6 2.0 %collective-permute-start.6 = (bf16[512,512]{1,0:T(8,128)(2,1)S(1)}, bf16[512,512]{1,0:T(8,128)(2,1)S(1)}, u32[]{:S(2)}, u32[]{:S(2)}) collective-permute-start(bf16[512,512]{1,0:T(8,128)(2,1)S(1)} %after.7.right_ref), channel_id=1, source_target_pairs={{0,1},{1,0},{2,3},{3,2},{4,5},{5,4},{6,7},{7,6},{8,9},{9,8},{10,11... | collective-permute-start | bytes 1572872 | tf_op jit(solution)/shard_map/ppermute | solution.py:378
  47.6 0.0 collective-permute-done.7.left_ref
  47.6 2.7 %middle.1 = (f32[1,512,1024]{2,1,0:T(8,128)}, f32[512,512]{1,0:T(8,128)S(1)}, bf16[2,512,256]{2,1,0:T(8,128)(2,1)S(1)}) custom-call(s32[256]{0:T(256)S(1)} %copy-done.6, bf16[528,512]{1,0:T(8,128)(2,1)S(1)} %collective-permute-done.7.left_ref, bf16[512,512]{1,0:T(8,128)(2,1)S(1)} %after.7.right_ref, f32[1,512,1024]{2,1,0:T(8,128)S(1)} %get-tuple-element.38.near_ref, ...), custom_call_target="tpu_custom_call" | custom-call | flops 1000 | bytes 8 | tf_op jit(solution)/shard_map/middle/pallas_call | solution.py:44
  50.4 0.0 collective-permute-done.6.right_ref
  50.4 2.2 %last.1 = f32[1,512,1024]{2,1,0:T(8,128)} custom-call(s32[256]{0:T(256)S(1)} %copy-done.6, bf16[512,512]{1,0:T(8,128)(2,1)S(1)} %collective-permute-done.6.right_ref, f32[512,512]{1,0:T(8,128)S(1)} %get-tuple-element.42.sum_ref, bf16[2,512,256]{2,1,0:T(8,128)(2,1)S(1)} %get-tuple-element.43.hot_ref, ...), custom_call_target="tpu_custom_call", output_to_operand_aliasing={{}: (4, {})} | custom-call | flops 1000 | bytes 8 | tf_op jit(solution)/shard_map/last/pallas_call | solution.py:44
  (14 shorter events, 0.0 us)
Async XLA Ops:
  0.6 34.5 %collective-permute-start.3 = (bf16[1,512,1024]{2,1,0:T(8,128)(2,1)}, bf16[1,512,1024]{2,1,0:T(8,128)(2,1)S(1)}, u32[]{:S(2)}, u32[]{:S(2)}) collective-permute-start(bf16[1,512,1024]{2,1,0:T(8,128)(2,1)} %here_ref.1), channel_id=1, source_target_pairs={{0,2},{2,4},{4,6},{6,8},{8,10},{10,12},{12,14},{14,16},{16,18},{18... | collective-permute-start | bytes 3145736 | tf_op jit(solution)/shard_map/ppermute | solution.py:351
  10.5 24.6 %collective-permute-start.4 = (bf16[1,512,1024]{2,1,0:T(8,128)(2,1)}, bf16[1,512,1024]{2,1,0:T(8,128)(2,1)S(1)}, u32[]{:S(2)}, u32[]{:S(2)}) collective-permute-start(bf16[1,512,1024]{2,1,0:T(8,128)(2,1)} %here_ref.1), channel_id=1, source_target_pairs={{1,3},{3,5},{5,7},{7,9},{9,11},{11,13},{13,15},{15,17},{17,19},{19... | collective-permute-start | bytes 3145736 | tf_op jit(solution)/shard_map/ppermute | solution.py:352
  12.5 2.1 %collective-permute-start = (s32[2,512]{1,0:T(2,128)}, s32[2,512]{1,0:T(2,128)S(1)}, u32[]{:S(2)}, u32[]{:S(2)}) collective-permute-start(s32[2,512]{1,0:T(2,128)} %pix_ref.3), channel_id=1, source_target_pairs={{0,1},{1,0},{2,3},{3,2},{4,5},{5,4},{6,7},{7,6},{8,9},{9,8},{10,11... | collective-permute-start | bytes 12296 | tf_op jit(solution)/shard_map/ppermute | solution.py:353
  14.6 2.2 %copy-start = (bf16[2,1024,1024]{2,1,0:T(8,128)(2,1)S(1)}, bf16[2,1024,1024]{2,1,0:T(8,128)(2,1)}, u32[]{:S(2)}) copy-start(bf16[2,1024,1024]{2,1,0:T(8,128)(2,1)} %weights_ref.5) | copy-start | bytes 12582916
  16.7 1.2 %copy-start.2 = (bf16[2,1024,256]{2,1,0:T(8,128)(2,1)S(1)}, bf16[2,1024,256]{2,1,0:T(8,128)(2,1)}, u32[]{:S(2)}) copy-start(bf16[2,1024,256]{2,1,0:T(8,128)(2,1)} %leaf_ref.2) | copy-start | bytes 3145732
  18.0 0.7 %copy-start.4 = (s32[2,512]{1,0:T(2,128)S(1)}, s32[2,512]{1,0:T(2,128)}, u32[]{:S(2)}) copy-start(s32[2,512]{1,0:T(2,128)} %pix_ref.3) | copy-start | bytes 12292
  18.7 2.8 %copy-start.3 = (bf16[1,1024,256]{2,1,0:T(8,128)(2,1)S(1)}, bf16[1,1024,256]{2,1,0:T(8,128)(2,1)}, u32[]{:S(2)}) copy-start(bf16[1,1024,256]{2,1,0:T(8,128)(2,1)} %leaf_ref.3) | copy-start | bytes 1572868
  18.7 2.8 %copy-start.5 = (s32[2,512]{1,0:T(2,128)S(1)}, s32[2,512]{1,0:T(2,128)}, u32[]{:S(2)}) copy-start(s32[2,512]{1,0:T(2,128)} %pix_ref.3) | copy-start | bytes 12292
  18.7 2.8 %copy-start.6 = (s32[256]{0:T(256)S(1)}, s32[256]{0:T(256)}, u32[]{:S(2)}) copy-start(s32[256]{0:T(256)} %ids_ref.9) | copy-start | bytes 3076
  18.7 2.8 %copy-start.7 = (s32[1,512]{1,0:T(1,128)S(1)}, s32[1,512]{1,0:T(1,128)}, u32[]{:S(2)}) copy-start(s32[1,512]{1,0:T(1,128)} %parent_pix_ref.1) | copy-start | bytes 6148
  26.1 9.1 %copy-start.8 = (bf16[1,512,1024]{2,1,0:T(8,128)(2,1)S(1)}, bf16[1,512,1024]{2,1,0:T(8,128)(2,1)}, u32[]{:S(2)}) copy-start(bf16[1,512,1024]{2,1,0:T(8,128)(2,1)} %here_ref.1) | copy-start | bytes 3145732
  26.1 17.9 %collective-permute-start.2 = (bf16[528,512]{1,0:T(8,128)(2,1)S(1)}, bf16[528,512]{1,0:T(8,128)(2,1)S(1)}, u32[]{:S(2)}, u32[]{:S(2)}) collective-permute-start(bf16[528,512]{1,0:T(8,128)(2,1)S(1)} %after.4.refs_1_), channel_id=1, source_target_pairs={{0,2},{2,4},{4,6},{6,8},{8,10},{10,12},{12,14},{14,16},{16,18},{18... | collective-permute-start | bytes 1622024 | tf_op jit(solution)/shard_map/ppermute | solution.py:360
  33.2 12.4 %collective-permute-start.1 = (bf16[512,512]{1,0:T(8,128)(2,1)S(1)}, bf16[512,512]{1,0:T(8,128)(2,1)S(1)}, u32[]{:S(2)}, u32[]{:S(2)}) collective-permute-start(bf16[512,512]{1,0:T(8,128)(2,1)S(1)} %after.5), channel_id=1, source_target_pairs={{0,2},{2,4},{4,6},{6,8},{8,10},{10,12},{12,14},{14,16},{16,18},{18... | collective-permute-start | bytes 1572872 | tf_op jit(solution)/shard_map/ppermute | solution.py:359
  35.1 2.2 %copy-start.1 = (bf16[2,1024,1024]{2,1,0:T(8,128)(2,1)S(1)}, bf16[2,1024,1024]{2,1,0:T(8,128)(2,1)}, u32[]{:S(2)}) copy-start(bf16[2,1024,1024]{2,1,0:T(8,128)(2,1)} %weights_ref.5) | copy-start | bytes 12582916
  37.0 3.8 %collective-permute-start.5 = (bf16[2,256,512]{2,1,0:T(8,128)(2,1)S(1)}, bf16[2,256,512]{2,1,0:T(8,128)(2,1)S(1)}, u32[]{:S(2)}, u32[]{:S(2)}) collective-permute-start(bf16[2,256,512]{2,1,0:T(8,128)(2,1)S(1)} %get-tuple-element.33), channel_id=1, source_target_pairs={{0,1},{1,0},{2,3},{3,2},{4,5},{5,4},{6,7},{7,6},{8,9},{9,8},{10,11... | collective-permute-start | bytes 1572872 | tf_op jit(solution)/shard_map/ppermute | solution.py:364
  44.0 3.6 %collective-permute-start.7 = (bf16[528,512]{1,0:T(8,128)(2,1)S(1)}, bf16[528,512]{1,0:T(8,128)(2,1)S(1)}, u32[]{:S(2)}, u32[]{:S(2)}) collective-permute-start(bf16[528,512]{1,0:T(8,128)(2,1)S(1)} %after.6.left_ref), channel_id=1, source_target_pairs={{0,1},{1,0},{2,3},{3,2},{4,5},{5,4},{6,7},{7,6},{8,9},{9,8},{10,11... | collective-permute-start | bytes 1622024 | tf_op jit(solution)/shard_map/ppermute | solution.py:368
  45.6 4.8 %collective-permute-start.6 = (bf16[512,512]{1,0:T(8,128)(2,1)S(1)}, bf16[512,512]{1,0:T(8,128)(2,1)S(1)}, u32[]{:S(2)}, u32[]{:S(2)}) collective-permute-start(bf16[512,512]{1,0:T(8,128)(2,1)S(1)} %after.7.right_ref), channel_id=1, source_target_pairs={{0,1},{1,0},{2,3},{3,2},{4,5},{5,4},{6,7},{7,6},{8,9},{9,8},{10,11... | collective-permute-start | bytes 1572872 | tf_op jit(solution)/shard_map/ppermute | solution.py:378
